TPU v7x, 32 devices: a whole 2x2x4 slice. The times are simulated.
32 devices in a mesh: rows: 4 (over y, x), cents: 8 (over z, core).
Axes of the slice: x: 2, y: 2, z: 4, core: 2. Of those that a mesh axis runs over, the one named last changes fastest.
Arguments:
- vectors: bfloat16 [2048, 1024], P(('rows', 'cents')), may hold values from -24 to 24, as said below
- centroids: bfloat16 [16384, 1024], P('cents'), may hold values from -0.1875 to 0.1875
Outputs:
- updated: bfloat16 [16384, 1024], P('cents', 'rows')
- masses: float32 [16384], P('cents')
Inputs may be any that keep to these rules, and one draw needn't show every extreme that they name: `vectors`: entries are real-valued and of order one, with rows of differing scales.
All inputs are finite; a program needn't handle non-finite values.
Results may differ from a plain program's by a relative error of at most 0.015.
Values may be sent and summed in bfloat16 or wider, within the bound.
A program may use at most 128 MiB of HBM per device.

v0:
```python
import jax
import jax.numpy as jnp
from jax import lax
from jax.sharding import PartitionSpec as P

ROUNDS = 3


SHARP = 0.75


def body(vectors, centroids):
    group = lax.all_gather(vectors, "cents", axis=0, tiled=True)
    logits = lax.dot_general(
        group, centroids, (((1,), (1,)), ((), ())), preferred_element_type=jnp.float32
    )
    weights = jnp.exp(SHARP * logits)
    groups_count = lax.axis_size("rows")
    shards_count = lax.axis_size("cents")
    target = group.shape[0] * groups_count / (centroids.shape[0] * shards_count)
    row_scale = jnp.ones((group.shape[0],), jnp.float32)
    col_scale = jnp.ones((centroids.shape[0],), jnp.float32)
    for step in range(ROUNDS):
        colmass = lax.psum(jnp.dot(row_scale, weights, precision=lax.Precision.HIGHEST), "rows")
        col_scale = target / colmass
        rowmass = lax.psum(jnp.dot(weights, col_scale, precision=lax.Precision.HIGHEST), "cents")
        row_scale = 1.0 / rowmass
    plan = weights * row_scale[:, None] * col_scale[None, :]
    masses = lax.psum(jnp.sum(plan, axis=0), "rows")
    plan_low = plan.astype(jnp.bfloat16)
    partial_value = lax.dot_general(
        plan_low, group, (((0,), (0,)), ((), ())), preferred_element_type=jnp.float32
    )
    share = centroids.shape[1] // groups_count
    offset = lax.axis_index("rows") * share
    totals = lax.psum(partial_value.astype(jnp.bfloat16), "rows").astype(jnp.float32)
    sums = lax.dynamic_slice_in_dim(totals, offset, share, 1)
    own_cols = lax.dynamic_slice_in_dim(centroids, offset, share, 1).astype(jnp.float32)
    updated = 0.5 * own_cols + 0.5 * sums / masses[:, None]
    return (updated.astype(jnp.bfloat16), masses)


def solution(mesh):
    return jax.shard_map(
        body,
        mesh=mesh,
        in_specs=(P(("rows", "cents"), None), P("cents", None)),
        out_specs=(P("cents", "rows"), P("cents")),
        check_vma=False,
    )
```

profile of v0, /device:TPU:0, one launch (start us, length us, event | category | flops | bytes accessed | tf_op | source)
XLA Modules:
  0.0 255.2 jit_solution(13400126395163109359)
XLA Ops:
  7.2 0.0 all-gather.2.cloned.1.call-start
  7.2 0.7 all-gather.2.cloned.1.call-update
  7.9 0.0 all-reduce.2.cloned.1.call-start
  7.9 26.5 %all-gather.2.cloned.1.call-done = bf16[512,1024]{1,0:T(8,128)(2,1)} async-done(((bf16[64,1024]{1,0:T(8,128)(2,1)}), bf16[512,1024]{1,0:T(8,128)(2,1)}) %all-gather.2.cloned.1.call-update) | async-done | bytes 1048592 | tf_op jit(solution)/shard_map/all_gather | solution.py:13
  34.4 4.9 %multiply_exponential_fusion = f32[512,2048]{1,0:T(8,128)S(1)} fusion(bf16[512,1024]{1,0:T(8,128)(2,1)} %all-gather.2.cloned.1.call-done, bf16[2048,1024]{1,0:T(8,128)(2,1)} %param.3), kind=kOutput, calls=%fused_computation.1 | convolution fusion | flops 2148532224 | bytes 9437184 | tf_op jit(solution)/shard_map/dot_general | solution.py:14
  39.4 1.9 copy-done
  41.3 2.1 fusion.5
  43.4 10.0 %psum.56 = f32[2048]{0:T(1024)S(1)} all-reduce(f32[2048]{0:T(1024)S(1)} %bitcast.30), channel_id=1, replica_groups=mesh['rows'=4,'cents'=8] {'rows'}, use_global_device_ids=true, to_apply=%region_0.0 | all-reduce | flops 2048 | bytes 16384 | tf_op jit(solution)/shard_map/psum | solution.py:24
  53.4 5.8 %fusion.8 = f32[1,512]{1,0:T(1,128)S(1)} fusion(f32[512,2048]{1,0:T(8,128)} %copy-done, f32[2048,1]{0,1:T(1,128)S(1)} %bitcast.26), kind=kOutput, calls=%fused_computation.17 | convolution fusion | flops 12582912 | bytes 4204544 | tf_op jit(solution)/shard_map/dot_general | solution.py:26
  59.1 13.6 %psum.57 = f32[512]{0:T(512)S(1)} all-reduce(f32[512]{0:T(512)S(1)} %bitcast.31), channel_id=1, replica_groups=mesh['rows'=4,'cents'=8] {'cents'}, use_global_device_ids=true, to_apply=%region_1.0 | all-reduce | flops 512 | bytes 4096 | tf_op jit(solution)/shard_map/psum | solution.py:26
  72.7 4.3 %fusion.9 = f32[1,2048]{1,0:T(1,128)S(1)} fusion(f32[512,1]{0,1:T(1,128)S(1)} %bitcast.32, f32[512,2048]{1,0:T(8,128)} %copy-done), kind=kOutput, calls=%fused_computation.18 | convolution fusion | flops 12582912 | bytes 4204544 | tf_op jit(solution)/shard_map/dot_general | solution.py:24
  77.0 8.2 %psum.58 = f32[2048]{0:T(1024)S(1)} all-reduce(f32[2048]{0:T(1024)S(1)} %bitcast.27), channel_id=1, replica_groups=mesh['rows'=4,'cents'=8] {'rows'}, use_global_device_ids=true, to_apply=%region_2.0 | all-reduce | flops 2048 | bytes 16384 | tf_op jit(solution)/shard_map/psum | solution.py:24
  85.3 5.8 %fusion.10 = f32[1,512]{1,0:T(1,128)S(1)} fusion(f32[512,2048]{1,0:T(8,128)} %copy-done, f32[2048,1]{0,1:T(1,128)S(1)} %bitcast.28), kind=kOutput, calls=%fused_computation.19 | convolution fusion | flops 12582912 | bytes 4204544 | tf_op jit(solution)/shard_map/dot_general | solution.py:26
  91.0 13.6 %psum.59 = f32[512]{0:T(512)S(1)} all-reduce(f32[512]{0:T(512)S(1)} %bitcast.33), channel_id=1, replica_groups=mesh['rows'=4,'cents'=8] {'cents'}, use_global_device_ids=true, to_apply=%region_3.0 | all-reduce | flops 512 | bytes 4096 | tf_op jit(solution)/shard_map/psum | solution.py:26
  104.6 4.4 %fusion.11 = f32[1,2048]{1,0:T(1,128)S(1)} fusion(f32[512,1]{0,1:T(1,128)S(1)} %bitcast.34, f32[512,2048]{1,0:T(8,128)} %copy-done), kind=kOutput, calls=%fused_computation.20 | convolution fusion | flops 12582912 | bytes 4204544 | tf_op jit(solution)/shard_map/dot_general | solution.py:24
  109.0 9.1 %psum.60 = f32[2048]{0:T(1024)S(1)} all-reduce(f32[2048]{0:T(1024)S(1)} %bitcast.29), channel_id=1, replica_groups=mesh['rows'=4,'cents'=8] {'rows'}, use_global_device_ids=true, to_apply=%region_4.0 | all-reduce | flops 2048 | bytes 16384 | tf_op jit(solution)/shard_map/psum | solution.py:24
  118.1 5.8 %fusion.12 = f32[1,512]{1,0:T(1,128)S(1)} fusion(f32[512,2048]{1,0:T(8,128)} %copy-done, f32[2048,1]{0,1:T(1,128)S(1)} %bitcast.25), kind=kOutput, calls=%fused_computation.21 | convolution fusion | flops 12582912 | bytes 4204544 | tf_op jit(solution)/shard_map/dot_general | solution.py:26
  123.9 13.6 %psum.61 = f32[512]{0:T(512)S(1)} all-reduce(f32[512]{0:T(512)S(1)} %bitcast.35), channel_id=1, replica_groups=mesh['rows'=4,'cents'=8] {'cents'}, use_global_device_ids=true, to_apply=%region_5.0 | all-reduce | flops 512 | bytes 4096 | tf_op jit(solution)/shard_map/psum | solution.py:26
  137.5 6.6 %convolution_convert_fusion = bf16[2048,1024]{1,0:T(8,128)(2,1)} fusion(bf16[512,1024]{1,0:T(8,128)(2,1)S(1)} %copy-done.2, f32[512,2048]{1,0:T(8,128)} %copy-done, f32[2048]{0:T(1024)S(1)} %broadcast_divide_fusion, f32[512]{0:T(512)S(1)} %broadcast_divide_fusion.5), kind=kOutput, calls=%fused_computation.2 | convolution fusion | flops 2152726528 | bytes 9447424 | tf_op jit(solution)/shard_map/dot_general | solution.py:31
  144.1 0.0 all-reduce.2.cloned.1.call-update
  144.2 2.7 %fusion = f32[2048]{0:T(1024)S(1)} fusion(f32[512,2048]{1,0:T(8,128)} %copy-done, f32[2048]{0:T(1024)S(1)} %broadcast_divide_fusion, f32[512]{0:T(512)S(1)} %broadcast_divide_fusion.5), kind=kLoop, calls=%fused_computation.3 | loop fusion | flops 3143680 | bytes 4212736 | tf_op jit(solution)/shard_map/reduce_sum | solution.py:29
  146.9 8.6 %psum.63 = f32[2048]{0:T(1024)S(1)} all-reduce(f32[2048]{0:T(1024)S(1)} %fusion), channel_id=1, replica_groups=mesh['rows'=4,'cents'=8] {'rows'}, use_global_device_ids=true, to_apply=%region_8.0 | all-reduce | flops 2048 | bytes 16384 | tf_op jit(solution)/shard_map/psum | solution.py:29
  155.4 89.9 %all-reduce.2.cloned.1.call-done = bf16[2048,1024]{1,0:T(8,128)(2,1)} async-done(((bf16[2048,1024]{1,0:T(8,128)(2,1)}), bf16[2048,1024]{1,0:T(8,128)(2,1)}) %all-reduce.2.cloned.1.call-update) | async-done | bytes 4194320 | tf_op jit(solution)/shard_map/psum | solution.py:36
  245.4 3.0 %add_convert_fusion = bf16[2048,256]{1,0:T(8,128)(2,1)} fusion(bf16[2048,1024]{1,0:T(8,128)(2,1)} %all-reduce.2.cloned.1.call-done, s32[]{:T(128)S(6)} %select_n.4, f32[2048]{0:T(1024)S(1)} %psum.63, bf16[2048,1024]{1,0:T(8,128)(2,1)} %param.3), kind=kLoop, calls=%fused_computation.5 | loop fusion | flops 3670016 | bytes 3153924 | tf_op jit(solution)/shard_map/convert_element_type | solution.py:40
  (11 shorter events, 0.0 us)
Async XLA Ops:
  7.2 27.3 %all-gather.2.cloned.1.call-start = ((), (), s32[]{:S(2)}) async-start(), calls=%async_computation | async-start | bytes 1179648 | tf_op jit(solution)/shard_map/all_gather | solution.py:13
  7.9 237.5 %all-reduce.2.cloned.1.call-start = ((), (), s32[]{:S(2)}) async-start(), calls=%async_computation.1 | async-start | bytes 8388608 | tf_op jit(solution)/shard_map/psum | solution.py:36
  39.4 1.9 copy-start
  104.6 32.9 %copy-start.2 = (bf16[512,1024]{1,0:T(8,128)(2,1)S(1)}, bf16[512,1024]{1,0:T(8,128)(2,1)}, u32[]{:S(2)}) copy-start(bf16[512,1024]{1,0:T(8,128)(2,1)} %all-gather.2.cloned.1.call-done) | copy-start | bytes 3145732
  155.4 93.0 %copy-start.1 = (f32[2048]{0:T(1024)}, f32[2048]{0:T(1024)S(1)}, u32[]{:S(2)}) copy-start(f32[2048]{0:T(1024)S(1)} %psum.63) | copy-start | bytes 24580
Sparse Core Ops, SparseCore 0:
  9.6 24.7 all-gather.1
  144.3 101.0 all-reduce.1
where the time goes:
time: 256 us; the launch traced here: 255 us
  waiting for transfers between devices  117 us (46%)
  blocking collectives  76.7 us (30%)
  matrix products  39.6 us (15%)
  between operations  14.1 us (6%)
  other arithmetic  5.74 us (2%)
    psum x1, waiting for transfers between devices, body(): lax.psum(partial_value.astype(jnp.bfloat16), 'rows').astype(jnp.float32)  89.9 us
    psum x3, blocking collectives, body(): lax.psum(jnp.dot(weights, col_scale, precision=lax.Precision.HIGHEST), 'c...  40.8 us
    psum x3, blocking collectives, body(): lax.psum(jnp.dot(row_scale, weights, precision=lax.Precision.HIGHEST), 'r...  27.3 us
    all_gather x1, waiting for transfers between devices, body(): group = lax.all_gather(vectors, 'cents', axis=0, tiled=True)  26.5 us
    dot_general x3, matrix products, body(): jnp.dot(weights, col_scale, precision=lax.Precision.HIGHEST)  17.3 us
    dot_general x3, matrix products, body(): jnp.dot(row_scale, weights, precision=lax.Precision.HIGHEST)  10.7 us
    psum x1, blocking collectives, body(): masses = lax.psum(jnp.sum(plan, axis=0), 'rows')  8.57 us
    dot_general x1, matrix products, body(): lax.dot_general(plan_low, group, (((0,), (0,)), ((), ())), preferred_elem...  6.65 us
  transfers between devices with their start and end apart: 2, of which 2 were waited for; matrix products, arithmetic and copies ran while one was open for 1% of the time, Pallas kernels for 0%

commit v1 on v0

v1 whole, which is shorter than its diff:
```python
import functools

import jax
import jax.numpy as jnp
from jax import lax
from jax.experimental import pallas as pl
from jax.experimental.pallas import tpu as pltpu

ROUNDS = 3
SHARP = 0.75
R = 4
LANES = 128
MESH = pl.DeviceIdType.MESH


def flip(a, d):
    out, bit = a, 1
    while bit <= d:
        if d & bit:
            out = out + bit - 2 * bit * lax.rem(lax.div(out, bit), 2)
        bit *= 2
    return out


def kernel(shards, target, vec, cent_hbm, out, mass_out, v, w, plan, cent, colb, massb, massrow, outbuf,
           part_a, part_b, box_a, box_b,
           gsend, grecv, asend, arecv, bsend, brecv, osend, orecv, msend, mrecv, lsem):
    r, c = lax.axis_index("rows"), lax.axis_index("cents")
    z, k = lax.div(c, 2), lax.rem(c, 2)
    depth = shards // 2
    rows = vec.shape[0]
    half = rows // 2
    mine = cent.shape[0]
    batch = v.shape[0]
    chunk = R * rows
    tiles = batch // LANES

    plane = [(q, s) for q in range(R) for s in range(2) if (q, s) != (0, 0)]

    def plane_dev(q, s):
        return (flip(r, q), flip(c, s))

    def z_dev(e):
        return (r, flip(z, e) * 2 + k)

    barrier = pltpu.get_barrier_semaphore()
    for q, s in plane:
        pl.semaphore_signal(barrier, inc=1, device_id=plane_dev(q, s), device_id_type=MESH)
    for e in range(1, depth):
        pl.semaphore_signal(barrier, inc=1, device_id=z_dev(e), device_id_type=MESH)
    cent_in = pltpu.make_async_copy(
        cent_hbm.at[pl.ds(pl.multiple_of(r * mine, mine), mine), :], cent, lsem.at[0])
    cent_in.start()
    pl.semaphore_wait(barrier, len(plane) + depth - 1)

    sent = []

    def piece(cc, rr, part):
        base = (cc * R + rr) * rows
        if part == 2:
            return v.at[pl.ds(pl.multiple_of(base, rows), rows), :]
        return v.at[pl.ds(pl.multiple_of(base + part * half, half), half), :]

    def gsem(cc, rr, part):
        return grecv.at[(cc * R + rr) * 2 + (0 if part == 2 else part)]

    def send(cc, rr, part, dev, src=None):
        copy = pltpu.make_async_remote_copy(
            src_ref=piece(cc, rr, part) if src is None else src,
            dst_ref=piece(cc, rr, part),
            send_sem=gsend.at[len(sent)],
            recv_sem=gsem(cc, rr, part),
            device_id=dev, device_id_type=MESH)
        copy.start()
        sent.append(copy)

    def arrive(cc, rr, part):
        ref = piece(cc, rr, part)
        pltpu.make_async_remote_copy(
            src_ref=ref, dst_ref=ref, send_sem=gsend.at[0], recv_sem=gsem(cc, rr, part),
            device_id=plane_dev(0, 1), device_id_type=MESH).wait_recv()

    east, north, other = plane_dev(1, 0), plane_dev(2, 0), plane_dev(0, 1)
    rx, ry, rd = flip(r, 1), flip(r, 2), flip(r, 3)

    def column(d):
        cc = flip(z, d) * 2 + k
        if d:
            arrive(cc, r, 2)
        src = None if d else vec
        send(cc, r, 2, east, src)
        send(cc, r, 2, north, src)
        send(cc, r, 2, other, src)

    def relay(d):
        cc = flip(z, d) * 2 + k
        arrive(cc, rx, 2)
        send(cc, rx, 0, north)
        send(cc, rx, 2, other)
        arrive(cc, ry, 2)
        send(cc, ry, 1, east)
        send(cc, ry, 2, other)

    def corner(d):
        cc = flip(z, d) * 2 + k
        arrive(cc, rd, 0)
        arrive(cc, rd, 1)
        send(cc, rd, 2, other)

    def weigh(cc):
        start = pl.multiple_of(cc * chunk, chunk)
        logits = lax.dot_general(
            cent[...], v[pl.ds(start, chunk), :], (((1,), (1,)), ((), ())),
            preferred_element_type=jnp.float32)
        w[:, pl.ds(start, chunk)] = jnp.exp(SHARP * logits)

    own = pltpu.make_async_copy(vec, piece(c, r, 2), lsem.at[1])
    own.start()
    if depth > 1:
        send(c, r, 2, z_dev(1), vec)
    column(0)
    for e in range(2, depth):
        send(c, r, 2, z_dev(e), vec)
    own.wait()
    cent_in.wait()
    for d in range(depth):
        relay(d)
        if d + 1 < depth:
            column(d + 1)
        corner(d)
        weigh(flip(z, d) * 2 + k)
        if d:
            cc = flip(z, d - 1) * 2 + 1 - k
            for rr in range(R):
                arrive(cc, rr, 2)
            weigh(cc)
    cc = flip(z, depth - 1) * 2 + 1 - k
    for rr in range(R):
        arrive(cc, rr, 2)
    weigh(cc)

    row_scale = jnp.ones((1, batch), jnp.float32)
    for step in range(ROUNDS):
        scales = [jnp.broadcast_to(row_scale[:, t * LANES:(t + 1) * LANES], (8, LANES)) for t in range(tiles)]

        def block(i, totals):
            at = pl.ds(pl.multiple_of(i * 8, 8), 8)
            terms = [w[at, t * LANES:(t + 1) * LANES] for t in range(tiles)]
            sums = [a * b for a, b in zip(terms, scales)]
            while len(sums) > 1:
                sums = [a + b for a, b in zip(sums[::2], sums[1::2])] + ([sums[-1]] if len(sums) % 2 else [])
            mass = jnp.sum(sums[0], axis=1, keepdims=True)
            col = jnp.broadcast_to(target / mass, (8, LANES))
            colb[at, :] = col
            return tuple(total + a * col for total, a in zip(totals, terms))

        totals = lax.fori_loop(
            0, mine // 8, block, tuple(jnp.zeros((8, LANES), jnp.float32) for _ in range(tiles)), unroll=4)
        for t in range(tiles):
            part_a[step, :, t * LANES:(t + 1) * LANES] = jnp.sum(totals[t], axis=0, keepdims=True)

        copies = []
        for j, (q, s) in enumerate(plane):
            copy = pltpu.make_async_remote_copy(
                src_ref=part_a.at[step], dst_ref=box_a.at[step, j], send_sem=asend.at[step, j],
                recv_sem=arecv.at[step, j], device_id=plane_dev(q, s), device_id_type=MESH)
            copy.start()
            copies.append(copy)
        total = part_a[step]
        for j, copy in enumerate(copies):
            copy.wait_recv()
            total = total + box_a[step, j]
        sent.extend(copies)
        part_b[step] = total
        copies = []
        for e in range(1, depth):
            copy = pltpu.make_async_remote_copy(
                src_ref=part_b.at[step], dst_ref=box_b.at[step, e], send_sem=bsend.at[step, e],
                recv_sem=brecv.at[step, e], device_id=z_dev(e), device_id_type=MESH)
            copy.start()
            copies.append(copy)
        for e, copy in enumerate(copies):
            copy.wait_recv()
            total = total + box_b[step, e + 1]
        sent.extend(copies)
        row_scale = 1.0 / total

    scales = [jnp.broadcast_to(row_scale[:, t * LANES:(t + 1) * LANES], (16, LANES)) for t in range(tiles)]

    def block(i, carry):
        at = pl.ds(pl.multiple_of(i * 16, 16), 16)
        col = colb[at, :]
        mass = jnp.zeros((16, LANES), jnp.float32)
        for t in range(tiles):
            term = w[at, t * LANES:(t + 1) * LANES] * scales[t] * col
            mass = mass + term
            plan[at, t * LANES:(t + 1) * LANES] = term.astype(jnp.bfloat16)
        massb[at, :] = jnp.broadcast_to(jnp.sum(mass, axis=1, keepdims=True), (16, LANES))
        return carry

    lax.fori_loop(0, mine // 16, block, 0, unroll=2)

    width = out.shape[1]
    results = []
    for q in (3, 1, 2, 0):
        peer = flip(r, q)
        cols = pl.ds(pl.multiple_of(peer * width, width), width)
        sums = jnp.dot(plan[...], v[:, cols], preferred_element_type=jnp.float32)
        mass = jnp.concatenate([massb[...]] * (width // LANES), axis=1)
        outbuf[q] = (0.5 * cent[:, cols].astype(jnp.float32) + 0.5 * sums / mass).astype(jnp.bfloat16)
        dst = out.at[pl.ds(pl.multiple_of(r * mine, mine), mine), :]
        if q:
            copy = pltpu.make_async_remote_copy(
                src_ref=outbuf.at[q], dst_ref=dst, send_sem=osend.at[q], recv_sem=orecv.at[q],
                device_id=(peer, c), device_id_type=MESH)
        else:
            copy = pltpu.make_async_copy(outbuf.at[q], dst, lsem.at[2])
        copy.start()
        results.append((q, copy))

    massrow[...] = jnp.transpose(massb[...], (1, 0))[:8, :]
    mdst = mass_out.at[pl.ds(pl.multiple_of(r * 8, 8), 8), :]
    mcopies = []
    for q in range(1, R):
        copy = pltpu.make_async_remote_copy(
            src_ref=massrow, dst_ref=mdst, send_sem=msend.at[q], recv_sem=mrecv.at[q],
            device_id=(flip(r, q), c), device_id_type=MESH)
        copy.start()
        mcopies.append(copy)
    local = pltpu.make_async_copy(massrow, mdst, lsem.at[3])
    local.start()

    for copy in sent:
        copy.wait_send()
    local.wait()
    for copy in mcopies:
        copy.wait()
    for q, copy in results:
        copy.wait()


def body(vectors, centroids, shards):
    rows, embed = vectors.shape
    batch = rows * R * shards
    held = centroids.shape[0]
    mine = held // R
    width = embed // R
    target = batch / (held * shards)
    depth = shards // 2
    f32, bf16 = jnp.float32, jnp.bfloat16
    dma = pltpu.SemaphoreType.DMA
    updated, masses = pl.pallas_call(
        functools.partial(kernel, shards, target),
        out_shape=(jax.ShapeDtypeStruct((held, width), bf16), jax.ShapeDtypeStruct((R * 8, mine), f32)),
        in_specs=[pl.BlockSpec(memory_space=pltpu.VMEM), pl.BlockSpec(memory_space=pl.ANY)],
        out_specs=(pl.BlockSpec(memory_space=pl.ANY), pl.BlockSpec(memory_space=pl.ANY)),
        scratch_shapes=[
            pltpu.VMEM((batch, embed), bf16),
            pltpu.VMEM((mine, batch), f32),
            pltpu.VMEM((mine, batch), bf16),
            pltpu.VMEM((mine, embed), bf16),
            pltpu.VMEM((mine, LANES), f32),
            pltpu.VMEM((mine, LANES), f32),
            pltpu.VMEM((8, mine), f32),
            pltpu.VMEM((R, mine, width), bf16),
            pltpu.VMEM((ROUNDS, 1, batch), f32),
            pltpu.VMEM((ROUNDS, 1, batch), f32),
            pltpu.VMEM((ROUNDS, 2 * R - 1, 1, batch), f32),
            pltpu.VMEM((ROUNDS, depth, 1, batch), f32),
            dma((depth * 9,)), dma((shards * R * 2,)),
            dma((ROUNDS, 2 * R)), dma((ROUNDS, 2 * R)),
            dma((ROUNDS, depth)), dma((ROUNDS, depth)),
            dma((R,)), dma((R,)), dma((R,)), dma((R,)), dma((4,)),
        ],
        compiler_params=pltpu.CompilerParams(
            collective_id=0, has_side_effects=True, vmem_limit_bytes=56 * 1024 * 1024),
        cost_estimate=pl.CostEstimate(
            flops=4 * mine * batch * embed, bytes_accessed=2 * mine * embed * 4, transcendentals=mine * batch),
    )(vectors, centroids)
    return updated, masses.reshape(R, 8, mine)[:, 0, :].reshape(held)


def solution(mesh):
    from jax.sharding import PartitionSpec as P
    return jax.shard_map(
        functools.partial(body, shards=mesh.shape["cents"]),
        mesh=mesh,
        in_specs=(P(("rows", "cents"), None), P("cents", None)),
        out_specs=(P("cents", "rows"), P("cents")),
        check_vma=False,
    )
```

time: 256 us -> 85.2 us (0.33)
  waiting for transfers between devices: 117 us -> 0 us
  Pallas kernels: 0 us -> 80.6 us
  blocking collectives: 76.7 us -> 0 us
  matrix products: 39.6 us -> 0 us
  between operations: 14.1 us -> 0.64 us
  other arithmetic: 5.74 us -> 0 us
    psum x1 -> x0, waiting for transfers between devices: 89.9 us -> none  [body(): lax.psum(partial_value.astype(jnp.bfloat16), 'rows').astype(jnp.float32)]
    pallas_call x0 -> x1, Pallas kernels: none -> 80.6 us  [body(): pl.pallas_call(functools.partial(kernel, shards, target), out_shape=(jax....]
    psum x7 -> x0, blocking collectives: 76.7 us -> none  [the longest x3 40.8 us: body(): lax.psum(jnp.dot(weights, col_scale, precision=lax.Precision.HIGHEST), 'c...]
    dot_general x8 -> x0, matrix products: 39.6 us -> none  [the longest x3 17.3 us: body(): jnp.dot(weights, col_scale, precision=lax.Precision.HIGHEST)]
    all_gather x1 -> x0, waiting for transfers between devices: 26.5 us -> none  [body(): group = lax.all_gather(vectors, 'cents', axis=0, tiled=True)]
    convert_element_type x1 -> x0, other arithmetic: 3.02 us -> none  [body(): return (updated.astype(jnp.bfloat16), masses)]
    reduce_sum x1 -> x0, other arithmetic: 2.68 us -> none  [body(): masses = lax.psum(jnp.sum(plan, axis=0), 'rows')]
  transfers between devices with their start and end apart: 2 -> 0, of which waited for: 2 -> 0; matrix products, arithmetic and copies ran while one was open for 1% -> 0% of each run, Pallas kernels for 0% -> 0%
where the time goes in v1:
time: 85.2 us; the launch traced here: 84.9 us
  Pallas kernels  80.6 us (95%)
  local copies, waits for them, and re-layouts  3.7 us (4%)
    pallas_call x1, Pallas kernels, body(): pl.pallas_call(functools.partial(kernel, shards, target), out_shape=(jax....  80.6 us
    unnamed x1, local copies, waits for them, and re-layouts  2.26 us

profile of v1, /device:TPU:0, one launch (start us, length us, event | category | flops | bytes accessed | tf_op | source)
XLA Modules:
  0.0 84.9 jit_solution(1856667180228752525)
XLA Ops:
  0.6 80.6 %shard_map.41 = (bf16[2048,256]{1,0:T(8,128)(2,1)}, f32[32,512]{1,0:T(8,128)}) custom-call(bf16[64,1024]{1,0:T(8,128)(2,1)} %vec.1, bf16[2048,1024]{1,0:T(8,128)(2,1)} %cent_hbm.1), custom_call_target="tpu_custom_call" | custom-call | flops 4294967296 | bytes 4194304 | tf_op jit(solution)/shard_map/pallas_call | solution.py:252
  81.2 1.4 %slice.4 = f32[4,1,512]{2,1,0:T(1,128)} slice(f32[4,8,512]{2,1,0:T(8,128)} %bitcast.3), slice={[0:4], [0:1], [0:512]} | slice | bytes 16384 | tf_op jit(solution)/shard_map/slice | solution.py:280
  82.7 2.3 %copy.5 = bf16[2048,256]{1,0:T(8,128)(2,1)} copy(bf16[2048,256]{1,0:T(8,128)(2,1)} %get-tuple-element.8) | data formatting | bytes 2097152

commit v2 on v1

--- a/solution.py
+++ b/solution.py
@@ -112,8 +112,14 @@
         logits = lax.dot_general(
             cent[...], v[pl.ds(start, chunk), :], (((1,), (1,)), ((), ())),
             preferred_element_type=jnp.float32)
-        w[:, pl.ds(start, chunk)] = jnp.exp(SHARP * logits)
-
+        terms = jnp.exp(SHARP * logits)
+        w[:, pl.ds(start, chunk)] = terms
+        sums = terms[:, :LANES]
+        for t in range(1, chunk // LANES):
+            sums = sums + terms[:, t * LANES:(t + 1) * LANES]
+        massb[...] += sums
+
+    massb[...] = jnp.zeros_like(massb)
     own = pltpu.make_async_copy(vec, piece(c, r, 2), lsem.at[1])
     own.start()
     if depth > 1:
@@ -139,23 +145,29 @@
         arrive(cc, rr, 2)
     weigh(cc)
 
-    row_scale = jnp.ones((1, batch), jnp.float32)
     for step in range(ROUNDS):
-        scales = [jnp.broadcast_to(row_scale[:, t * LANES:(t + 1) * LANES], (8, LANES)) for t in range(tiles)]
-
-        def block(i, totals):
+        if step:
+            scales = [jnp.broadcast_to(row_scale[:, t * LANES:(t + 1) * LANES], (8, LANES)) for t in range(tiles)]
+
+            def col_block(i, carry):
+                at = pl.ds(pl.multiple_of(i * 8, 8), 8)
+                sums = [w[at, t * LANES:(t + 1) * LANES] * scales[t] for t in range(tiles)]
+                while len(sums) > 1:
+                    sums = [a + b for a, b in zip(sums[::2], sums[1::2])] + ([sums[-1]] if len(sums) % 2 else [])
+                massb[at, :] = sums[0]
+                return carry
+
+            lax.fori_loop(0, mine // 8, col_block, 0, unroll=8)
+        mass = jnp.sum(massb[...], axis=1, keepdims=True)
+        colb[...] = jnp.broadcast_to(target / mass, colb.shape)
+
+        def row_block(i, totals):
             at = pl.ds(pl.multiple_of(i * 8, 8), 8)
-            terms = [w[at, t * LANES:(t + 1) * LANES] for t in range(tiles)]
-            sums = [a * b for a, b in zip(terms, scales)]
-            while len(sums) > 1:
-                sums = [a + b for a, b in zip(sums[::2], sums[1::2])] + ([sums[-1]] if len(sums) % 2 else [])
-            mass = jnp.sum(sums[0], axis=1, keepdims=True)
-            col = jnp.broadcast_to(target / mass, (8, LANES))
-            colb[at, :] = col
-            return tuple(total + a * col for total, a in zip(totals, terms))
+            col = colb[at, :]
+            return tuple(total + w[at, t * LANES:(t + 1) * LANES] * col for t, total in enumerate(totals))
 
         totals = lax.fori_loop(
-            0, mine // 8, block, tuple(jnp.zeros((8, LANES), jnp.float32) for _ in range(tiles)), unroll=4)
+            0, mine // 8, row_block, tuple(jnp.zeros((8, LANES), jnp.float32) for _ in range(tiles)), unroll=8)
         for t in range(tiles):
             part_a[step, :, t * LANES:(t + 1) * LANES] = jnp.sum(totals[t], axis=0, keepdims=True)
 
@@ -195,10 +207,11 @@
             term = w[at, t * LANES:(t + 1) * LANES] * scales[t] * col
             mass = mass + term
             plan[at, t * LANES:(t + 1) * LANES] = term.astype(jnp.bfloat16)
-        massb[at, :] = jnp.broadcast_to(jnp.sum(mass, axis=1, keepdims=True), (16, LANES))
+        massb[at, :] = mass
         return carry
 
-    lax.fori_loop(0, mine // 16, block, 0, unroll=2)
+    lax.fori_loop(0, mine // 16, block, 0, unroll=4)
+    massb[...] = jnp.broadcast_to(jnp.sum(massb[...], axis=1, keepdims=True), massb.shape)
 
     width = out.shape[1]
     results = []
@@ -218,8 +231,8 @@
         copy.start()
         results.append((q, copy))
 
-    massrow[...] = jnp.transpose(massb[...], (1, 0))[:8, :]
-    mdst = mass_out.at[pl.ds(pl.multiple_of(r * 8, 8), 8), :]
+    massrow[...] = jnp.transpose(massb[...], (1, 0))[:1, :]
+    mdst = mass_out.at[r]
     mcopies = []
     for q in range(1, R):
         copy = pltpu.make_async_remote_copy(
@@ -249,9 +262,10 @@
     depth = shards // 2
     f32, bf16 = jnp.float32, jnp.bfloat16
     dma = pltpu.SemaphoreType.DMA
+    limit = 56 << 20
     updated, masses = pl.pallas_call(
         functools.partial(kernel, shards, target),
-        out_shape=(jax.ShapeDtypeStruct((held, width), bf16), jax.ShapeDtypeStruct((R * 8, mine), f32)),
+        out_shape=(jax.ShapeDtypeStruct((held, width), bf16), jax.ShapeDtypeStruct((R, 1, mine), f32)),
         in_specs=[pl.BlockSpec(memory_space=pltpu.VMEM), pl.BlockSpec(memory_space=pl.ANY)],
         out_specs=(pl.BlockSpec(memory_space=pl.ANY), pl.BlockSpec(memory_space=pl.ANY)),
         scratch_shapes=[
@@ -261,7 +275,7 @@
             pltpu.VMEM((mine, embed), bf16),
             pltpu.VMEM((mine, LANES), f32),
             pltpu.VMEM((mine, LANES), f32),
-            pltpu.VMEM((8, mine), f32),
+            pltpu.VMEM((1, mine), f32),
             pltpu.VMEM((R, mine, width), bf16),
             pltpu.VMEM((ROUNDS, 1, batch), f32),
             pltpu.VMEM((ROUNDS, 1, batch), f32),
@@ -273,11 +287,11 @@
             dma((R,)), dma((R,)), dma((R,)), dma((R,)), dma((4,)),
         ],
         compiler_params=pltpu.CompilerParams(
-            collective_id=0, has_side_effects=True, vmem_limit_bytes=56 * 1024 * 1024),
+            collective_id=0, has_side_effects=True, vmem_limit_bytes=limit),
         cost_estimate=pl.CostEstimate(
             flops=4 * mine * batch * embed, bytes_accessed=2 * mine * embed * 4, transcendentals=mine * batch),
     )(vectors, centroids)
-    return updated, masses.reshape(R, 8, mine)[:, 0, :].reshape(held)
+    return updated, masses.reshape(held)
 
 
 def solution(mesh):

time: 85.2 us -> 79.8 us (0.937)
  Pallas kernels: 80.6 us -> 75.4 us
    pallas_call x1, Pallas kernels: 80.6 us -> 75.4 us  [body(): pl.pallas_call(functools.partial(kernel, shards, target), out_shape=(jax....]
    slice x1 -> x0, local copies, waits for them, and re-layouts: 1.44 us -> none  [body(): return (updated, masses.reshape(R, 8, mine)[:, 0, :].reshape(held))]
    unnamed x1 -> x2, local copies, waits for them, and re-layouts: 2.26 us -> 3.56 us
where the time goes in v2:
time: 79.8 us; the launch traced here: 79.6 us
  Pallas kernels  75.4 us (94%)
  local copies, waits for them, and re-layouts  3.56 us (4%)
    pallas_call x1, Pallas kernels, body(): pl.pallas_call(functools.partial(kernel, shards, target), out_shape=(jax....  75.4 us
    unnamed x2, local copies, waits for them, and re-layouts  3.56 us

profile of v2, /device:TPU:0, one launch (start us, length us, event | category | flops | bytes accessed | tf_op | source)
XLA Modules:
  0.0 79.6 jit_solution(1163963360335145220)
XLA Ops:
  0.6 75.4 %shard_map.41 = (bf16[2048,256]{1,0:T(8,128)(2,1)}, f32[4,1,512]{2,1,0:T(1,128)}) custom-call(bf16[64,1024]{1,0:T(8,128)(2,1)} %vec.1, bf16[2048,1024]{1,0:T(8,128)(2,1)} %cent_hbm.1), custom_call_target="tpu_custom_call" | custom-call | flops 4294967296 | bytes 4194304 | tf_op jit(solution)/shard_map/pallas_call | solution.py:266
  76.0 2.3 %copy.6 = bf16[2048,256]{1,0:T(8,128)(2,1)} copy(bf16[2048,256]{1,0:T(8,128)(2,1)} %get-tuple-element.8) | data formatting | bytes 2097152
  78.3 1.3 %copy.7 = f32[2048]{0:T(1024)} copy(f32[2048]{0:T(1024)} %bitcast.1) | data formatting | bytes 16384

commit v3 on v2

--- a/solution.py
+++ b/solution.py
@@ -24,7 +24,7 @@
 
 def kernel(shards, target, vec, cent_hbm, out, mass_out, v, w, plan, cent, colb, massb, massrow, outbuf,
            part_a, part_b, box_a, box_b,
-           gsend, grecv, asend, arecv, bsend, brecv, osend, orecv, msend, mrecv, lsem):
+           gsend, psend, grecv, asend, arecv, bsend, brecv, osend, orecv, msend, mrecv, lsem):
     r, c = lax.axis_index("rows"), lax.axis_index("cents")
     z, k = lax.div(c, 2), lax.rem(c, 2)
     depth = shards // 2
@@ -83,17 +83,42 @@
     east, north, other = plane_dev(1, 0), plane_dev(2, 0), plane_dev(0, 1)
     rx, ry, rd = flip(r, 1), flip(r, 2), flip(r, 3)
 
+    line = depth == 4
+    inner = lax.rem(lax.div(z + 1, 2), 2)
+
+    def source(d):
+        if line and d >= 2:
+            return inner * flip(z, 5 - d) + (1 - inner) * flip(z, d)
+        return flip(z, d)
+
+    passed = []
+
+    def pass_on(cc, e, src=None):
+        n = len(passed)
+        copy = pltpu.make_async_remote_copy(
+            src_ref=piece(cc, r, 2) if src is None else src,
+            dst_ref=piece(cc, r, 2),
+            send_sem=psend.at[n], recv_sem=gsem(cc, r, 2),
+            device_id=z_dev(e), device_id_type=MESH)
+        passed.append(copy)
+
+        @pl.when(inner == 1)
+        def _():
+            copy.start()
+
     def column(d):
-        cc = flip(z, d) * 2 + k
+        cc = source(d) * 2 + k
         if d:
             arrive(cc, r, 2)
+            if line:
+                pass_on(cc, 3 if d == 1 else 1)
         src = None if d else vec
         send(cc, r, 2, east, src)
         send(cc, r, 2, north, src)
         send(cc, r, 2, other, src)
 
     def relay(d):
-        cc = flip(z, d) * 2 + k
+        cc = source(d) * 2 + k
         arrive(cc, rx, 2)
         send(cc, rx, 0, north)
         send(cc, rx, 2, other)
@@ -102,7 +127,7 @@
         send(cc, ry, 2, other)
 
     def corner(d):
-        cc = flip(z, d) * 2 + k
+        cc = source(d) * 2 + k
         arrive(cc, rd, 0)
         arrive(cc, rd, 1)
         send(cc, rd, 2, other)
@@ -124,26 +149,30 @@
     own.start()
     if depth > 1:
         send(c, r, 2, z_dev(1), vec)
+    if line:
+        pass_on(c, 3, vec)
     column(0)
-    for e in range(2, depth):
-        send(c, r, 2, z_dev(e), vec)
+    if not line:
+        for e in range(2, depth):
+            send(c, r, 2, z_dev(e), vec)
     own.wait()
     cent_in.wait()
+
+    def partner(d):
+        cc = source(d) * 2 + 1 - k
+        for rr in range(R):
+            arrive(cc, rr, 2)
+        weigh(cc)
+
     for d in range(depth):
         relay(d)
         if d + 1 < depth:
             column(d + 1)
+        if d:
+            partner(d - 1)
         corner(d)
-        weigh(flip(z, d) * 2 + k)
-        if d:
-            cc = flip(z, d - 1) * 2 + 1 - k
-            for rr in range(R):
-                arrive(cc, rr, 2)
-            weigh(cc)
-    cc = flip(z, depth - 1) * 2 + 1 - k
-    for rr in range(R):
-        arrive(cc, rr, 2)
-    weigh(cc)
+        weigh(source(d) * 2 + k)
+    partner(depth - 1)
 
     for step in range(ROUNDS):
         if step:
@@ -245,6 +274,11 @@
 
     for copy in sent:
         copy.wait_send()
+    if passed:
+        @pl.when(inner == 1)
+        def _():
+            for copy in passed:
+                copy.wait_send()
     local.wait()
     for copy in mcopies:
         copy.wait()
@@ -262,7 +296,7 @@
     depth = shards // 2
     f32, bf16 = jnp.float32, jnp.bfloat16
     dma = pltpu.SemaphoreType.DMA
-    limit = 56 << 20
+    limit = 51 << 20
     updated, masses = pl.pallas_call(
         functools.partial(kernel, shards, target),
         out_shape=(jax.ShapeDtypeStruct((held, width), bf16), jax.ShapeDtypeStruct((R, 1, mine), f32)),
@@ -281,7 +315,7 @@
             pltpu.VMEM((ROUNDS, 1, batch), f32),
             pltpu.VMEM((ROUNDS, 2 * R - 1, 1, batch), f32),
             pltpu.VMEM((ROUNDS, depth, 1, batch), f32),
-            dma((depth * 9,)), dma((shards * R * 2,)),
+            dma((depth * 9,)), dma((4,)), dma((shards * R * 2,)),
             dma((ROUNDS, 2 * R)), dma((ROUNDS, 2 * R)),
             dma((ROUNDS, depth)), dma((ROUNDS, depth)),
             dma((R,)), dma((R,)), dma((R,)), dma((R,)), dma((4,)),

time: 79.8 us -> 77.6 us (0.972)
  Pallas kernels: 75.4 us -> 74.3 us
  local copies, waits for them, and re-layouts: 3.56 us -> 2.47 us
    unnamed x2 -> x4, local copies, waits for them, and re-layouts: 3.56 us -> 2.47 us
    pallas_call x1, Pallas kernels: 75.4 us -> 74.3 us  [body(): pl.pallas_call(functools.partial(kernel, shards, target), out_shape=(jax....]
where the time goes in v3:
time: 77.6 us; the launch traced here: 77.4 us
  Pallas kernels  74.3 us (96%)
  local copies, waits for them, and re-layouts  2.47 us (3%)
    pallas_call x1, Pallas kernels, body(): pl.pallas_call(functools.partial(kernel, shards, target), out_shape=(jax....  74.3 us
    unnamed x4, local copies, waits for them, and re-layouts  2.47 us

profile of v3, /device:TPU:0, one launch (start us, length us, event | category | flops | bytes accessed | tf_op | source)
XLA Modules:
  0.0 77.4 jit_solution(14632496468816870198)
XLA Ops:
  0.6 0.0 copy-start
  0.6 0.9 %copy-done = bf16[64,1024]{1,0:T(8,128)(2,1)S(1)} copy-done((bf16[64,1024]{1,0:T(8,128)(2,1)S(1)}, bf16[64,1024]{1,0:T(8,128)(2,1)}, u32[]{:S(2)}) %copy-start) | copy-done | bytes 131096
  1.5 74.3 %shard_map.41 = (bf16[2048,256]{1,0:T(8,128)(2,1)S(1)}, f32[4,1,512]{2,1,0:T(1,128)S(1)}) custom-call(bf16[64,1024]{1,0:T(8,128)(2,1)S(1)} %copy-done, bf16[2048,1024]{1,0:T(8,128)(2,1)} %cent_hbm.1), custom_call_target="tpu_custom_call" | custom-call | flops 4294967296 | bytes 4194304 | tf_op jit(solution)/shard_map/pallas_call | solution.py:300
  75.8 1.0 %copy.6 = bf16[2048,256]{1,0:T(8,128)(2,1)} copy(bf16[2048,256]{1,0:T(8,128)(2,1)S(1)} %get-tuple-element.8) | data formatting | bytes 2097152
  76.8 0.6 copy.7
Async XLA Ops:
  0.6 0.9 %copy-start = (bf16[64,1024]{1,0:T(8,128)(2,1)S(1)}, bf16[64,1024]{1,0:T(8,128)(2,1)}, u32[]{:S(2)}) copy-start(bf16[64,1024]{1,0:T(8,128)(2,1)} %vec.1) | copy-start | bytes 393220

commit v4 on v3

--- a/solution.py
+++ b/solution.py
@@ -164,10 +164,12 @@
             arrive(cc, rr, 2)
         weigh(cc)
 
+    if depth > 1:
+        column(1)
     for d in range(depth):
         relay(d)
-        if d + 1 < depth:
-            column(d + 1)
+        if d + 2 < depth:
+            column(d + 2)
         if d:
             partner(d - 1)
         corner(d)
@@ -176,7 +178,7 @@
 
     for step in range(ROUNDS):
         if step:
-            scales = [jnp.broadcast_to(row_scale[:, t * LANES:(t + 1) * LANES], (8, LANES)) for t in range(tiles)]
+            scales = [jnp.broadcast_to(row_scale[t:t + 1, :], (8, LANES)) for t in range(tiles)]
 
             def col_block(i, carry):
                 at = pl.ds(pl.multiple_of(i * 8, 8), 8)
@@ -197,9 +199,9 @@
 
         totals = lax.fori_loop(
             0, mine // 8, row_block, tuple(jnp.zeros((8, LANES), jnp.float32) for _ in range(tiles)), unroll=8)
-        for t in range(tiles):
-            part_a[step, :, t * LANES:(t + 1) * LANES] = jnp.sum(totals[t], axis=0, keepdims=True)
-
+        total = jnp.concatenate([jnp.sum(part, axis=0, keepdims=True) for part in totals], axis=0)
+
+        part_a[step] = total.astype(jnp.bfloat16)
         copies = []
         for j, (q, s) in enumerate(plane):
             copy = pltpu.make_async_remote_copy(
@@ -207,12 +209,11 @@
                 recv_sem=arecv.at[step, j], device_id=plane_dev(q, s), device_id_type=MESH)
             copy.start()
             copies.append(copy)
-        total = part_a[step]
         for j, copy in enumerate(copies):
             copy.wait_recv()
-            total = total + box_a[step, j]
+            total = total + box_a[step, j].astype(jnp.float32)
         sent.extend(copies)
-        part_b[step] = total
+        part_b[step] = total.astype(jnp.bfloat16)
         copies = []
         for e in range(1, depth):
             copy = pltpu.make_async_remote_copy(
@@ -222,11 +223,11 @@
             copies.append(copy)
         for e, copy in enumerate(copies):
             copy.wait_recv()
-            total = total + box_b[step, e + 1]
+            total = total + box_b[step, e + 1].astype(jnp.float32)
         sent.extend(copies)
         row_scale = 1.0 / total
 
-    scales = [jnp.broadcast_to(row_scale[:, t * LANES:(t + 1) * LANES], (16, LANES)) for t in range(tiles)]
+    scales = [jnp.broadcast_to(row_scale[t:t + 1, :], (16, LANES)) for t in range(tiles)]
 
     def block(i, carry):
         at = pl.ds(pl.multiple_of(i * 16, 16), 16)
@@ -294,6 +295,7 @@
     width = embed // R
     target = batch / (held * shards)
     depth = shards // 2
+    tiles = batch // LANES
     f32, bf16 = jnp.float32, jnp.bfloat16
     dma = pltpu.SemaphoreType.DMA
     limit = 51 << 20
@@ -311,10 +313,10 @@
             pltpu.VMEM((mine, LANES), f32),
             pltpu.VMEM((1, mine), f32),
             pltpu.VMEM((R, mine, width), bf16),
-            pltpu.VMEM((ROUNDS, 1, batch), f32),
-            pltpu.VMEM((ROUNDS, 1, batch), f32),
-            pltpu.VMEM((ROUNDS, 2 * R - 1, 1, batch), f32),
-            pltpu.VMEM((ROUNDS, depth, 1, batch), f32),
+            pltpu.VMEM((ROUNDS, tiles, LANES), bf16),
+            pltpu.VMEM((ROUNDS, tiles, LANES), bf16),
+            pltpu.VMEM((ROUNDS, 2 * R - 1, tiles, LANES), bf16),
+            pltpu.VMEM((ROUNDS, depth, tiles, LANES), bf16),
             dma((depth * 9,)), dma((4,)), dma((shards * R * 2,)),
             dma((ROUNDS, 2 * R)), dma((ROUNDS, 2 * R)),
             dma((ROUNDS, depth)), dma((ROUNDS, depth)),

time: 77.6 us -> 74.1 us (0.955)
  Pallas kernels: 74.3 us -> 70.8 us
    pallas_call x1, Pallas kernels: 74.3 us -> 70.8 us  [body(): pl.pallas_call(functools.partial(kernel, shards, target), out_shape=(jax....]
where the time goes in v4:
time: 74.1 us; the launch traced here: 73.9 us
  Pallas kernels  70.8 us (96%)
  local copies, waits for them, and re-layouts  2.47 us (3%)
    pallas_call x1, Pallas kernels, body(): pl.pallas_call(functools.partial(kernel, shards, target), out_shape=(jax....  70.8 us
    unnamed x4, local copies, waits for them, and re-layouts  2.47 us

profile of v4, /device:TPU:0, one launch (start us, length us, event | category | flops | bytes accessed | tf_op | source)
XLA Modules:
  0.0 73.9 jit_solution(12230657466007769157)
XLA Ops:
  0.6 0.0 copy-start
  0.6 0.9 %copy-done = bf16[64,1024]{1,0:T(8,128)(2,1)S(1)} copy-done((bf16[64,1024]{1,0:T(8,128)(2,1)S(1)}, bf16[64,1024]{1,0:T(8,128)(2,1)}, u32[]{:S(2)}) %copy-start) | copy-done | bytes 131096
  1.5 70.8 %shard_map.41 = (bf16[2048,256]{1,0:T(8,128)(2,1)S(1)}, f32[4,1,512]{2,1,0:T(1,128)S(1)}) custom-call(bf16[64,1024]{1,0:T(8,128)(2,1)S(1)} %copy-done, bf16[2048,1024]{1,0:T(8,128)(2,1)} %cent_hbm.1), custom_call_target="tpu_custom_call" | custom-call | flops 4294967296 | bytes 4194304 | tf_op jit(solution)/shard_map/pallas_call | solution.py:302
  72.4 1.0 %copy.6 = bf16[2048,256]{1,0:T(8,128)(2,1)} copy(bf16[2048,256]{1,0:T(8,128)(2,1)S(1)} %get-tuple-element.8) | data formatting | bytes 2097152
  73.3 0.6 copy.7
Async XLA Ops:
  0.6 0.9 %copy-start = (bf16[64,1024]{1,0:T(8,128)(2,1)S(1)}, bf16[64,1024]{1,0:T(8,128)(2,1)}, u32[]{:S(2)}) copy-start(bf16[64,1024]{1,0:T(8,128)(2,1)} %vec.1) | copy-start | bytes 393220

commit v5 on v4

--- a/solution.py
+++ b/solution.py
@@ -35,7 +35,7 @@
     chunk = R * rows
     tiles = batch // LANES
 
-    plane = [(q, s) for q in range(R) for s in range(2) if (q, s) != (0, 0)]
+    plane = [(3, 1), (3, 0), (2, 1), (1, 1), (2, 0), (1, 0), (0, 1)]
 
     def plane_dev(q, s):
         return (flip(r, q), flip(c, s))
@@ -166,10 +166,12 @@
 
     if depth > 1:
         column(1)
+    relay(0)
     for d in range(depth):
-        relay(d)
         if d + 2 < depth:
             column(d + 2)
+        if d + 1 < depth:
+            relay(d + 1)
         if d:
             partner(d - 1)
         corner(d)
@@ -209,21 +211,21 @@
                 recv_sem=arecv.at[step, j], device_id=plane_dev(q, s), device_id_type=MESH)
             copy.start()
             copies.append(copy)
-        for j, copy in enumerate(copies):
+        for j, copy in reversed(list(enumerate(copies))):
             copy.wait_recv()
             total = total + box_a[step, j].astype(jnp.float32)
         sent.extend(copies)
         part_b[step] = total.astype(jnp.bfloat16)
         copies = []
-        for e in range(1, depth):
+        for e in reversed(range(1, depth)):
             copy = pltpu.make_async_remote_copy(
                 src_ref=part_b.at[step], dst_ref=box_b.at[step, e], send_sem=bsend.at[step, e],
                 recv_sem=brecv.at[step, e], device_id=z_dev(e), device_id_type=MESH)
             copy.start()
             copies.append(copy)
-        for e, copy in enumerate(copies):
+        for e, copy in zip(range(1, depth), reversed(copies)):
             copy.wait_recv()
-            total = total + box_b[step, e + 1].astype(jnp.float32)
+            total = total + box_b[step, e].astype(jnp.float32)
         sent.extend(copies)
         row_scale = 1.0 / total
 

time: 74.1 us -> 72.4 us (0.977)
  Pallas kernels: 70.8 us -> 69.2 us
    pallas_call x1, Pallas kernels: 70.8 us -> 69.2 us  [body(): pl.pallas_call(functools.partial(kernel, shards, target), out_shape=(jax....]
where the time goes in v5:
time: 72.4 us; the launch traced here: 72.3 us
  Pallas kernels  69.2 us (96%)
  local copies, waits for them, and re-layouts  2.47 us (3%)
    pallas_call x1, Pallas kernels, body(): pl.pallas_call(functools.partial(kernel, shards, target), out_shape=(jax....  69.2 us
    unnamed x4, local copies, waits for them, and re-layouts  2.47 us

profile of v5, /device:TPU:0, one launch (start us, length us, event | category | flops | bytes accessed | tf_op | source)
XLA Modules:
  0.0 72.3 jit_solution(14720266517677330106)
XLA Ops:
  0.6 0.0 copy-start
  0.6 0.9 %copy-done = bf16[64,1024]{1,0:T(8,128)(2,1)S(1)} copy-done((bf16[64,1024]{1,0:T(8,128)(2,1)S(1)}, bf16[64,1024]{1,0:T(8,128)(2,1)}, u32[]{:S(2)}) %copy-start) | copy-done | bytes 131096
  1.5 69.2 %shard_map.41 = (bf16[2048,256]{1,0:T(8,128)(2,1)S(1)}, f32[4,1,512]{2,1,0:T(1,128)S(1)}) custom-call(bf16[64,1024]{1,0:T(8,128)(2,1)S(1)} %copy-done, bf16[2048,1024]{1,0:T(8,128)(2,1)} %cent_hbm.1), custom_call_target="tpu_custom_call" | custom-call | flops 4294967296 | bytes 4194304 | tf_op jit(solution)/shard_map/pallas_call | solution.py:304
  70.7 1.0 %copy.6 = bf16[2048,256]{1,0:T(8,128)(2,1)} copy(bf16[2048,256]{1,0:T(8,128)(2,1)S(1)} %get-tuple-element.8) | data formatting | bytes 2097152
  71.7 0.6 copy.7
Async XLA Ops:
  0.6 0.9 %copy-start = (bf16[64,1024]{1,0:T(8,128)(2,1)S(1)}, bf16[64,1024]{1,0:T(8,128)(2,1)}, u32[]{:S(2)}) copy-start(bf16[64,1024]{1,0:T(8,128)(2,1)} %vec.1) | copy-start | bytes 393220

commit v6 on v5

--- a/solution.py
+++ b/solution.py
@@ -93,12 +93,12 @@
 
     passed = []
 
-    def pass_on(cc, e, src=None):
+    def pass_on(cc, e, part, src=None):
         n = len(passed)
         copy = pltpu.make_async_remote_copy(
-            src_ref=piece(cc, r, 2) if src is None else src,
-            dst_ref=piece(cc, r, 2),
-            send_sem=psend.at[n], recv_sem=gsem(cc, r, 2),
+            src_ref=piece(cc, r, part) if src is None else src,
+            dst_ref=piece(cc, r, part),
+            send_sem=psend.at[n], recv_sem=gsem(cc, r, part),
             device_id=z_dev(e), device_id_type=MESH)
         passed.append(copy)
 
@@ -106,24 +106,35 @@
         def _():
             copy.start()
 
+    halves = [vec.at[pl.ds(0, half), :], vec.at[pl.ds(half, half), :]]
+
     def column(d):
         cc = source(d) * 2 + k
-        if d:
-            arrive(cc, r, 2)
-            if line:
-                pass_on(cc, 3 if d == 1 else 1)
-        src = None if d else vec
-        send(cc, r, 2, east, src)
-        send(cc, r, 2, north, src)
-        send(cc, r, 2, other, src)
+        for part, first in ((0, east), (1, north)):
+            src = None if d else halves[part]
+            if d:
+                arrive(cc, r, part)
+                if line:
+                    pass_on(cc, 3 if d == 1 else 1, part)
+            else:
+                if depth > 1:
+                    send(cc, r, part, z_dev(1), src)
+                if line:
+                    pass_on(cc, 3, part, src)
+            send(cc, r, part, first, src)
+        for part, second in ((1, east), (0, north)):
+            send(cc, r, part, second, None if d else halves[part])
+        send(cc, r, 2, other, None if d else vec)
 
     def relay(d):
         cc = source(d) * 2 + k
-        arrive(cc, rx, 2)
+        arrive(cc, rx, 0)
         send(cc, rx, 0, north)
+        arrive(cc, ry, 1)
+        send(cc, ry, 1, east)
+        arrive(cc, rx, 1)
         send(cc, rx, 2, other)
-        arrive(cc, ry, 2)
-        send(cc, ry, 1, east)
+        arrive(cc, ry, 0)
         send(cc, ry, 2, other)
 
     def corner(d):
@@ -147,14 +158,11 @@
     massb[...] = jnp.zeros_like(massb)
     own = pltpu.make_async_copy(vec, piece(c, r, 2), lsem.at[1])
     own.start()
-    if depth > 1:
-        send(c, r, 2, z_dev(1), vec)
-    if line:
-        pass_on(c, 3, vec)
     column(0)
     if not line:
         for e in range(2, depth):
-            send(c, r, 2, z_dev(e), vec)
+            for part in range(2):
+                send(c, r, part, z_dev(e), halves[part])
     own.wait()
     cent_in.wait()
 
@@ -319,7 +327,7 @@
             pltpu.VMEM((ROUNDS, tiles, LANES), bf16),
             pltpu.VMEM((ROUNDS, 2 * R - 1, tiles, LANES), bf16),
             pltpu.VMEM((ROUNDS, depth, tiles, LANES), bf16),
-            dma((depth * 9,)), dma((4,)), dma((shards * R * 2,)),
+            dma((depth * 12,)), dma((8,)), dma((shards * R * 2,)),
             dma((ROUNDS, 2 * R)), dma((ROUNDS, 2 * R)),
             dma((ROUNDS, depth)), dma((ROUNDS, depth)),
             dma((R,)), dma((R,)), dma((R,)), dma((R,)), dma((4,)),

time: 72.4 us -> 71.9 us (level)
  no operation moved by 1% of the time
where the time goes in v6:
time: 71.9 us; the launch traced here: 71.8 us
  Pallas kernels  68.6 us (95%)
  local copies, waits for them, and re-layouts  2.47 us (3%)
    pallas_call x1, Pallas kernels, body(): pl.pallas_call(functools.partial(kernel, shards, target), out_shape=(jax....  68.6 us
    unnamed x4, local copies, waits for them, and re-layouts  2.47 us

profile of v6, /device:TPU:0, one launch (start us, length us, event | category | flops | bytes accessed | tf_op | source)
XLA Modules:
  0.0 71.8 jit_solution(9894416783787764736)
XLA Ops:
  0.6 0.0 copy-start
  0.6 0.9 %copy-done = bf16[64,1024]{1,0:T(8,128)(2,1)S(1)} copy-done((bf16[64,1024]{1,0:T(8,128)(2,1)S(1)}, bf16[64,1024]{1,0:T(8,128)(2,1)}, u32[]{:S(2)}) %copy-start) | copy-done | bytes 131096
  1.5 68.6 %shard_map.41 = (bf16[2048,256]{1,0:T(8,128)(2,1)S(1)}, f32[4,1,512]{2,1,0:T(1,128)S(1)}) custom-call(bf16[64,1024]{1,0:T(8,128)(2,1)S(1)} %copy-done, bf16[2048,1024]{1,0:T(8,128)(2,1)} %cent_hbm.1), custom_call_target="tpu_custom_call" | custom-call | flops 4294967296 | bytes 4194304 | tf_op jit(solution)/shard_map/pallas_call | solution.py:312
  70.2 1.0 %copy.6 = bf16[2048,256]{1,0:T(8,128)(2,1)} copy(bf16[2048,256]{1,0:T(8,128)(2,1)S(1)} %get-tuple-element.8) | data formatting | bytes 2097152
  71.2 0.6 copy.7
Async XLA Ops:
  0.6 0.9 %copy-start = (bf16[64,1024]{1,0:T(8,128)(2,1)S(1)}, bf16[64,1024]{1,0:T(8,128)(2,1)}, u32[]{:S(2)}) copy-start(bf16[64,1024]{1,0:T(8,128)(2,1)} %vec.1) | copy-start | bytes 393220

commit v7 on v6

--- a/solution.py
+++ b/solution.py
@@ -10,6 +10,7 @@
 SHARP = 0.75
 R = 4
 LANES = 128
+PIECES = 8
 MESH = pl.DeviceIdType.MESH
 
 
@@ -24,7 +25,7 @@
 
 def kernel(shards, target, vec, cent_hbm, out, mass_out, v, w, plan, cent, colb, massb, massrow, outbuf,
            part_a, part_b, box_a, box_b,
-           gsend, psend, grecv, asend, arecv, bsend, brecv, osend, orecv, msend, mrecv, lsem):
+           gsend, psend, qrecv, grecv, asend, arecv, bsend, brecv, osend, orecv, msend, mrecv, lsem):
     r, c = lax.axis_index("rows"), lax.axis_index("cents")
     z, k = lax.div(c, 2), lax.rem(c, 2)
     depth = shards // 2
@@ -55,27 +56,31 @@
 
     sent = []
 
-    def piece(cc, rr, part):
+    line = depth == 4
+    embed = vec.shape[1]
+    cut = embed - LANES if line else embed
+
+    def piece(cc, rr, part, width):
         base = (cc * R + rr) * rows
         if part == 2:
-            return v.at[pl.ds(pl.multiple_of(base, rows), rows), :]
-        return v.at[pl.ds(pl.multiple_of(base + part * half, half), half), :]
+            return v.at[pl.ds(pl.multiple_of(base, rows), rows), pl.ds(0, width)]
+        return v.at[pl.ds(pl.multiple_of(base + part * half, half), half), pl.ds(0, width)]
 
     def gsem(cc, rr, part):
         return grecv.at[(cc * R + rr) * 2 + (0 if part == 2 else part)]
 
-    def send(cc, rr, part, dev, src=None):
+    def send(cc, rr, part, dev, width, src=None):
         copy = pltpu.make_async_remote_copy(
-            src_ref=piece(cc, rr, part) if src is None else src,
-            dst_ref=piece(cc, rr, part),
+            src_ref=piece(cc, rr, part, width) if src is None else src,
+            dst_ref=piece(cc, rr, part, width),
             send_sem=gsend.at[len(sent)],
             recv_sem=gsem(cc, rr, part),
             device_id=dev, device_id_type=MESH)
         copy.start()
         sent.append(copy)
 
-    def arrive(cc, rr, part):
-        ref = piece(cc, rr, part)
+    def arrive(cc, rr, part, width):
+        ref = piece(cc, rr, part, width)
         pltpu.make_async_remote_copy(
             src_ref=ref, dst_ref=ref, send_sem=gsend.at[0], recv_sem=gsem(cc, rr, part),
             device_id=plane_dev(0, 1), device_id_type=MESH).wait_recv()
@@ -83,7 +88,6 @@
     east, north, other = plane_dev(1, 0), plane_dev(2, 0), plane_dev(0, 1)
     rx, ry, rd = flip(r, 1), flip(r, 2), flip(r, 3)
 
-    line = depth == 4
     inner = lax.rem(lax.div(z + 1, 2), 2)
 
     def source(d):
@@ -96,8 +100,8 @@
     def pass_on(cc, e, part, src=None):
         n = len(passed)
         copy = pltpu.make_async_remote_copy(
-            src_ref=piece(cc, r, part) if src is None else src,
-            dst_ref=piece(cc, r, part),
+            src_ref=piece(cc, r, part, cut) if src is None else src,
+            dst_ref=piece(cc, r, part, cut),
             send_sem=psend.at[n], recv_sem=gsem(cc, r, part),
             device_id=z_dev(e), device_id_type=MESH)
         passed.append(copy)
@@ -107,41 +111,66 @@
             copy.start()
 
     halves = [vec.at[pl.ds(0, half), :], vec.at[pl.ds(half, half), :]]
+    parts = [vec.at[pl.ds(0, half), pl.ds(0, cut)], vec.at[pl.ds(half, half), pl.ds(0, cut)]]
 
     def column(d):
         cc = source(d) * 2 + k
+        width = cut if d else embed
         for part, first in ((0, east), (1, north)):
             src = None if d else halves[part]
             if d:
-                arrive(cc, r, part)
+                arrive(cc, r, part, cut)
                 if line:
                     pass_on(cc, 3 if d == 1 else 1, part)
             else:
                 if depth > 1:
-                    send(cc, r, part, z_dev(1), src)
+                    send(cc, r, part, z_dev(1), cut, parts[part])
                 if line:
-                    pass_on(cc, 3, part, src)
-            send(cc, r, part, first, src)
+                    pass_on(cc, 3, part, parts[part])
+            send(cc, r, part, first, width, src)
         for part, second in ((1, east), (0, north)):
-            send(cc, r, part, second, None if d else halves[part])
-        send(cc, r, 2, other, None if d else vec)
+            send(cc, r, part, second, width, None if d else halves[part])
+        send(cc, r, 2, other, width, None if d else vec)
 
     def relay(d):
         cc = source(d) * 2 + k
-        arrive(cc, rx, 0)
-        send(cc, rx, 0, north)
-        arrive(cc, ry, 1)
-        send(cc, ry, 1, east)
-        arrive(cc, rx, 1)
-        send(cc, rx, 2, other)
-        arrive(cc, ry, 0)
-        send(cc, ry, 2, other)
+        width = cut if d else embed
+        arrive(cc, rx, 0, width)
+        send(cc, rx, 0, north, width)
+        arrive(cc, ry, 1, width)
+        send(cc, ry, 1, east, width)
+        arrive(cc, rx, 1, width)
+        send(cc, rx, 2, other, width)
+        arrive(cc, ry, 0, width)
+        send(cc, ry, 2, other, width)
 
     def corner(d):
         cc = source(d) * 2 + k
-        arrive(cc, rd, 0)
-        arrive(cc, rd, 1)
-        send(cc, rd, 2, other)
+        width = cut if d else embed
+        arrive(cc, rd, 0, width)
+        arrive(cc, rd, 1, width)
+        send(cc, rd, 2, other, width)
+
+    def strip_copy(cc, dev, sem):
+        ref = v.at[pl.ds(pl.multiple_of(cc * chunk, chunk), chunk), pl.ds(cut, LANES)]
+        return pltpu.make_async_remote_copy(
+            src_ref=ref, dst_ref=ref, send_sem=sem, recv_sem=qrecv.at[cc],
+            device_id=dev, device_id_type=MESH)
+
+    def strip(d):
+        cc = source(d) * 2 + k
+        if d:
+            strip_copy(cc, other, gsend.at[0]).wait_recv()
+        on = strip_copy(cc, z_dev(1 if d > 1 else 3), psend.at[len(passed)])
+        passed.append(on)
+
+        @pl.when(inner == 1)
+        def _():
+            on.start()
+
+        copy = strip_copy(cc, other if d else z_dev(1), gsend.at[len(sent)])
+        copy.start()
+        sent.append(copy)
 
     def weigh(cc):
         start = pl.multiple_of(cc * chunk, chunk)
@@ -156,20 +185,22 @@
         massb[...] += sums
 
     massb[...] = jnp.zeros_like(massb)
-    own = pltpu.make_async_copy(vec, piece(c, r, 2), lsem.at[1])
+    own = pltpu.make_async_copy(vec, piece(c, r, 2, embed), lsem.at[1])
     own.start()
     column(0)
     if not line:
         for e in range(2, depth):
             for part in range(2):
-                send(c, r, part, z_dev(e), halves[part])
+                send(c, r, part, z_dev(e), embed, halves[part])
     own.wait()
     cent_in.wait()
 
     def partner(d):
         cc = source(d) * 2 + 1 - k
         for rr in range(R):
-            arrive(cc, rr, 2)
+            arrive(cc, rr, 2, cut if d else embed)
+        if line and d:
+            strip_copy(cc, other, gsend.at[0]).wait_recv()
         weigh(cc)
 
     if depth > 1:
@@ -183,6 +214,8 @@
         if d:
             partner(d - 1)
         corner(d)
+        if line:
+            strip(d)
         weigh(source(d) * 2 + k)
     partner(depth - 1)
 
@@ -297,6 +330,18 @@
         copy.wait()
 
 
+def finish(updated, masses, updated_out, masses_out, sem):
+    step = updated.shape[0] // PIECES
+    copies = [pltpu.make_async_copy(masses, masses_out, sem.at[PIECES])]
+    for i in range(PIECES):
+        at = pl.ds(i * step, step)
+        copies.append(pltpu.make_async_copy(updated.at[at, :], updated_out.at[at, :], sem.at[i]))
+    for copy in copies:
+        copy.start()
+    for copy in copies:
+        copy.wait()
+
+
 def body(vectors, centroids, shards):
     rows, embed = vectors.shape
     batch = rows * R * shards
@@ -308,7 +353,7 @@
     tiles = batch // LANES
     f32, bf16 = jnp.float32, jnp.bfloat16
     dma = pltpu.SemaphoreType.DMA
-    limit = 51 << 20
+    limit = 56 << 20
     updated, masses = pl.pallas_call(
         functools.partial(kernel, shards, target),
         out_shape=(jax.ShapeDtypeStruct((held, width), bf16), jax.ShapeDtypeStruct((R, 1, mine), f32)),
@@ -327,7 +372,7 @@
             pltpu.VMEM((ROUNDS, tiles, LANES), bf16),
             pltpu.VMEM((ROUNDS, 2 * R - 1, tiles, LANES), bf16),
             pltpu.VMEM((ROUNDS, depth, tiles, LANES), bf16),
-            dma((depth * 12,)), dma((8,)), dma((shards * R * 2,)),
+            dma((depth * 12,)), dma((12,)), dma((shards,)), dma((shards * R * 2,)),
             dma((ROUNDS, 2 * R)), dma((ROUNDS, 2 * R)),
             dma((ROUNDS, depth)), dma((ROUNDS, depth)),
             dma((R,)), dma((R,)), dma((R,)), dma((R,)), dma((4,)),
@@ -337,6 +382,15 @@
         cost_estimate=pl.CostEstimate(
             flops=4 * mine * batch * embed, bytes_accessed=2 * mine * embed * 4, transcendentals=mine * batch),
     )(vectors, centroids)
+    updated, masses = pl.pallas_call(
+        finish,
+        out_shape=(jax.ShapeDtypeStruct(updated.shape, bf16), jax.ShapeDtypeStruct(masses.shape, f32)),
+        in_specs=[pl.BlockSpec(memory_space=pl.ANY)] * 2,
+        out_specs=(pl.BlockSpec(memory_space=pl.ANY),) * 2,
+        scratch_shapes=[dma((PIECES + 1,))],
+        compiler_params=pltpu.CompilerParams(vmem_limit_bytes=limit),
+        cost_estimate=pl.CostEstimate(flops=0, bytes_accessed=2 * held * width * 2, transcendentals=0),
+    )(updated, masses)
     return updated, masses.reshape(held)
 
 

time: 71.9 us -> 104 us (1.45)
  Pallas kernels: 68.6 us -> 103 us
  local copies, waits for them, and re-layouts: 2.47 us -> 0 us
    pallas_call x0 -> x1, Pallas kernels: none -> 33.2 us  [body(): pl.pallas_call(finish, out_shape=(jax.ShapeDtypeStruct(updated.shape, bf1...]
    unnamed x4 -> x0, local copies, waits for them, and re-layouts: 2.47 us -> none
    pallas_call x1, Pallas kernels: 68.6 us -> 69.9 us  [body(): pl.pallas_call(functools.partial(kernel, shards, target), out_shape=(jax....]
where the time goes in v7:
time: 104 us
  Pallas kernels  103 us (99%)
    pallas_call x1, Pallas kernels, body(): pl.pallas_call(functools.partial(kernel, shards, target), out_shape=(jax....  69.9 us
    pallas_call x1, Pallas kernels, body(): pl.pallas_call(finish, out_shape=(jax.ShapeDtypeStruct(updated.shape, bf1...  33.2 us

profile of v7, /device:TPU:0, one launch (start us, length us, event | category | flops | bytes accessed | tf_op | source)
XLA Modules:
  0.0 103.7 jit_solution(10704340350956974180)
XLA Ops:
  0.6 69.9 %shard_map.41 = (bf16[2048,256]{1,0:T(8,128)(2,1)}, f32[4,1,512]{2,1,0:T(1,128)}) custom-call(bf16[64,1024]{1,0:T(8,128)(2,1)} %vec.1, bf16[2048,1024]{1,0:T(8,128)(2,1)} %cent_hbm.1), custom_call_target="tpu_custom_call" | custom-call | flops 4294967296 | bytes 4194304 | tf_op jit(solution)/shard_map/pallas_call | solution.py:357
  70.5 33.2 %shard_map.42 = (bf16[2048,256]{1,0:T(8,128)(2,1)}, f32[4,1,512]{2,1,0:T(1,128)}) custom-call(bf16[2048,256]{1,0:T(8,128)(2,1)} %get-tuple-element.6.updated, f32[4,1,512]{2,1,0:T(1,128)} %get-tuple-element.7.masses), custom_call_target="tpu_custom_call" | custom-call | bytes 2097152 | tf_op jit(solution)/shard_map/pallas_call | solution.py:385

commit v8 on v7

--- a/solution.py
+++ b/solution.py
@@ -353,7 +353,7 @@
     tiles = batch // LANES
     f32, bf16 = jnp.float32, jnp.bfloat16
     dma = pltpu.SemaphoreType.DMA
-    limit = 56 << 20
+    limit = 51 << 20
     updated, masses = pl.pallas_call(
         functools.partial(kernel, shards, target),
         out_shape=(jax.ShapeDtypeStruct((held, width), bf16), jax.ShapeDtypeStruct((R, 1, mine), f32)),
@@ -388,7 +388,7 @@
         in_specs=[pl.BlockSpec(memory_space=pl.ANY)] * 2,
         out_specs=(pl.BlockSpec(memory_space=pl.ANY),) * 2,
         scratch_shapes=[dma((PIECES + 1,))],
-        compiler_params=pltpu.CompilerParams(vmem_limit_bytes=limit),
+        compiler_params=pltpu.CompilerParams(vmem_limit_bytes=2 << 20),
         cost_estimate=pl.CostEstimate(flops=0, bytes_accessed=2 * held * width * 2, transcendentals=0),
     )(updated, masses)
     return updated, masses.reshape(held)

time: 104 us -> 71.6 us (0.69)
  Pallas kernels: 103 us -> 69.9 us
    pallas_call x1, Pallas kernels: 33.2 us -> 1.04 us  [body(): pl.pallas_call(finish, out_shape=(jax.ShapeDtypeStruct(updated.shape, bf1...]
where the time goes in v8:
time: 71.6 us; the launch traced here: 71.4 us
  Pallas kernels  69.9 us (98%)
  local copies, waits for them, and re-layouts  0.9 us (1%)
    pallas_call x1, Pallas kernels, body(): pl.pallas_call(functools.partial(kernel, shards, target), out_shape=(jax....  68.8 us

profile of v8, /device:TPU:0, one launch (start us, length us, event | category | flops | bytes accessed | tf_op | source)
XLA Modules:
  0.0 71.4 jit_solution(17732158018093679292)
XLA Ops:
  0.6 0.0 copy-start
  0.6 0.9 %copy-done = bf16[64,1024]{1,0:T(8,128)(2,1)S(1)} copy-done((bf16[64,1024]{1,0:T(8,128)(2,1)S(1)}, bf16[64,1024]{1,0:T(8,128)(2,1)}, u32[]{:S(2)}) %copy-start) | copy-done | bytes 131096
  1.5 68.8 %shard_map.41 = (bf16[2048,256]{1,0:T(8,128)(2,1)S(1)}, f32[4,1,512]{2,1,0:T(1,128)S(1)}) custom-call(bf16[64,1024]{1,0:T(8,128)(2,1)S(1)} %copy-done, bf16[2048,1024]{1,0:T(8,128)(2,1)} %cent_hbm.1), custom_call_target="tpu_custom_call" | custom-call | flops 4294967296 | bytes 4194304 | tf_op jit(solution)/shard_map/pallas_call | solution.py:357
  70.4 1.0 %shard_map.42 = (bf16[2048,256]{1,0:T(8,128)(2,1)}, f32[4,1,512]{2,1,0:T(1,128)}) custom-call(bf16[2048,256]{1,0:T(8,128)(2,1)S(1)} %get-tuple-element.6.updated, f32[4,1,512]{2,1,0:T(1,128)S(1)} %get-tuple-element.7.masses), custom_call_target="tpu_custom_call" | custom-call | bytes 2097152 | tf_op jit(solution)/shard_map/pallas_call | solution.py:385
Async XLA Ops:
  0.6 0.9 %copy-start = (bf16[64,1024]{1,0:T(8,128)(2,1)S(1)}, bf16[64,1024]{1,0:T(8,128)(2,1)}, u32[]{:S(2)}) copy-start(bf16[64,1024]{1,0:T(8,128)(2,1)} %vec.1) | copy-start | bytes 393220

commit v9 on v8

--- a/solution.py
+++ b/solution.py
@@ -10,7 +10,7 @@
 SHARP = 0.75
 R = 4
 LANES = 128
-PIECES = 8
+PIECES = 2
 MESH = pl.DeviceIdType.MESH
 
 
@@ -231,7 +231,7 @@
                 massb[at, :] = sums[0]
                 return carry
 
-            lax.fori_loop(0, mine // 8, col_block, 0, unroll=8)
+            lax.fori_loop(0, mine // 8, col_block, 0, unroll=16)
         mass = jnp.sum(massb[...], axis=1, keepdims=True)
         colb[...] = jnp.broadcast_to(target / mass, colb.shape)
 
@@ -241,7 +241,7 @@
             return tuple(total + w[at, t * LANES:(t + 1) * LANES] * col for t, total in enumerate(totals))
 
         totals = lax.fori_loop(
-            0, mine // 8, row_block, tuple(jnp.zeros((8, LANES), jnp.float32) for _ in range(tiles)), unroll=8)
+            0, mine // 8, row_block, tuple(jnp.zeros((8, LANES), jnp.float32) for _ in range(tiles)), unroll=16)
         total = jnp.concatenate([jnp.sum(part, axis=0, keepdims=True) for part in totals], axis=0)
 
         part_a[step] = total.astype(jnp.bfloat16)

time: 71.6 us -> 71.4 us (level)
  no operation moved by 1% of the time
where the time goes in v9:
time: 71.4 us; the launch traced here: 71.2 us
  Pallas kernels  69.7 us (98%)
  local copies, waits for them, and re-layouts  0.9 us (1%)
    pallas_call x1, Pallas kernels, body(): pl.pallas_call(functools.partial(kernel, shards, target), out_shape=(jax....  68.7 us

profile of v9, /device:TPU:0, one launch (start us, length us, event | category | flops | bytes accessed | tf_op | source)
XLA Modules:
  0.0 71.2 jit_solution(8725737370758242016)
XLA Ops:
  0.6 0.0 copy-start
  0.6 0.9 %copy-done = bf16[64,1024]{1,0:T(8,128)(2,1)S(1)} copy-done((bf16[64,1024]{1,0:T(8,128)(2,1)S(1)}, bf16[64,1024]{1,0:T(8,128)(2,1)}, u32[]{:S(2)}) %copy-start) | copy-done | bytes 131096
  1.5 68.7 %shard_map.41 = (bf16[2048,256]{1,0:T(8,128)(2,1)S(1)}, f32[4,1,512]{2,1,0:T(1,128)S(1)}) custom-call(bf16[64,1024]{1,0:T(8,128)(2,1)S(1)} %copy-done, bf16[2048,1024]{1,0:T(8,128)(2,1)} %cent_hbm.1), custom_call_target="tpu_custom_call" | custom-call | flops 4294967296 | bytes 4194304 | tf_op jit(solution)/shard_map/pallas_call | solution.py:357
  70.2 1.0 %shard_map.42 = (bf16[2048,256]{1,0:T(8,128)(2,1)}, f32[4,1,512]{2,1,0:T(1,128)}) custom-call(bf16[2048,256]{1,0:T(8,128)(2,1)S(1)} %get-tuple-element.6.updated, f32[4,1,512]{2,1,0:T(1,128)S(1)} %get-tuple-element.7.masses), custom_call_target="tpu_custom_call" | custom-call | bytes 2097152 | tf_op jit(solution)/shard_map/pallas_call | solution.py:385
Async XLA Ops:
  0.6 0.9 %copy-start = (bf16[64,1024]{1,0:T(8,128)(2,1)S(1)}, bf16[64,1024]{1,0:T(8,128)(2,1)}, u32[]{:S(2)}) copy-start(bf16[64,1024]{1,0:T(8,128)(2,1)} %vec.1) | copy-start | bytes 393220
